TPU v7x, 128 devices: a whole 4x4x4 slice. The times are simulated.
128 devices in a mesh: rows: 16 (over y, z_lo, core), cols: 8 (over z_hi, x).
Axes of the slice: x: 4, y: 4, z: 4 (z_hi: 2, z_lo: 2; z = z_hi * 2 + z_lo), core: 2. Of those that a mesh axis runs over, the one named last changes fastest.
Arguments:
- tokens: bfloat16 [512, 1024, 256], P('rows', 'cols'), may hold values from -6 to 6
- norm_gains: float32 [4, 256], replicated, may hold values from 0.5 to 1.5
- qkv_weight: bfloat16 [2, 256, 768], replicated, may hold values from -10 to 10
- out_weight: bfloat16 [2, 256, 256], replicated, may hold values from -0.375 to 0.375
- up_weight: bfloat16 [2, 256, 1024], replicated, may hold values from -0.375 to 0.375
- down_weight: bfloat16 [2, 1024, 256], replicated, may hold values from -0.1875 to 0.1875
Outputs:
- block_output: bfloat16 [512, 1024, 256], P('rows', 'cols')
All inputs are finite; a program needn't handle non-finite values.
Results may differ from a plain program's by a relative error of at most 0.018.
Values may be sent and summed in bfloat16 or wider, within the bound.
A program may use at most 128 MiB of HBM per device.

v0:
```python
import math

import jax
import jax.numpy as jnp
from jax import lax
from jax.experimental import pallas as pl
from jax.experimental.pallas import tpu as pltpu
from jax.sharding import PartitionSpec as P

HEADS = 8
EPSILON = 1e-06
CHANNELS = 256
HEAD_DIM = CHANNELS // HEADS
SCORE_SCALE = math.log2(math.e) / math.sqrt(HEAD_DIM)
BANDS = 4
BAND_ROWS = 8
BREADTH = 128
BAND_TOKENS = BAND_ROWS * BREADTH
PEERS = 64
CHUNK = BAND_TOKENS // PEERS
BLOCK = 256
MESH = pl.DeviceIdType.MESH


def layer_norm(x, gain):
    centred = x - jnp.mean(x, axis=-1, keepdims=True)
    spread = jnp.mean(centred * centred, axis=-1, keepdims=True)
    return (centred * lax.rsqrt(spread + EPSILON) * gain).astype(jnp.bfloat16)


def dot(a, b):
    return jnp.dot(a, b, preferred_element_type=jnp.float32)


def feed_forward(mix, gain, up, down):
    normed = layer_norm(mix, gain)
    units = dot(normed, up)
    hidden = (0.5 * units) * (1.0 + lax.erf(units * math.sqrt(0.5)))
    return mix + dot(hidden.astype(jnp.bfloat16), down)


def spread_heads(x, masks):
    return jnp.concatenate(
        [x[16 * t : 16 * t + 16] * masks[h] for t in range(4) for h in range(HEADS)], axis=0
    )


def segment_max(x, lane):
    for d in (1, 2, 4, 8):
        partner = jnp.where((lane & d) == 0, pltpu.roll(x, 128 - d, 1), pltpu.roll(x, d, 1))
        x = jnp.maximum(x, partner)
    return x


def attend(qkv, masks, ones, lane):
    query = qkv[:, :CHANNELS]
    keys = spread_heads(qkv[:, CHANNELS : 2 * CHANNELS], masks)
    values = spread_heads(qkv[:, 2 * CHANNELS :], masks)
    scores = lax.dot_general(
        query, keys, (((1,), (1,)), ((), ())), preferred_element_type=jnp.float32
    )
    parts = [scores[:, 128 * t : 128 * t + 128] for t in range(4)]
    top = jnp.maximum(jnp.maximum(parts[0], parts[1]), jnp.maximum(parts[2], parts[3]))
    top = segment_max(top, lane)
    weights = jnp.concatenate(
        [jnp.exp2((p - top) * SCORE_SCALE).astype(jnp.bfloat16) for p in parts], axis=1
    )
    total = dot(weights, ones)
    return (dot(weights, values) / total).astype(jnp.bfloat16)


def attention(normed, qkv_weight, out_weight, masks, ones, lane):
    qkv = dot(normed, qkv_weight).astype(jnp.bfloat16)
    attended = [
        attend(qkv[64 * w : 64 * w + 64], masks, ones, lane) for w in range(normed.shape[0] // 64)
    ]
    return dot(jnp.concatenate(attended, axis=0), out_weight)


def kernel(
    tokens, gains, qkv_weight, out_weight, up_weight, down_weight, out,
    sent, recv, terms, back, regroup, ungroup,
    sent_sem, recv_sem, terms_sem, back_sem,
):
    row, col = lax.axis_index("rows"), lax.axis_index("cols")
    core = lax.rem(row, 2)
    me = (row // 2) * 8 + col

    def peer(k):
        p = lax.rem(me + k, PEERS)
        return p, (2 * (p // 8) + core, lax.rem(p, 8))

    barrier = pltpu.get_barrier_semaphore()

    @pl.loop(1, PEERS)
    def _(k):
        pl.semaphore_signal(barrier, inc=1, device_id=peer(k)[1], device_id_type=MESH)

    pl.semaphore_wait(barrier, PEERS - 1)

    def chunk(ref, b, p):
        return ref.at[b, pl.ds(pl.multiple_of(p * CHUNK, CHUNK), CHUNK)]

    def exchange(src, dst, b, src_sem, dst_sem):
        @pl.loop(1, PEERS)
        def _(k):
            p, device = peer(k)
            pltpu.make_async_remote_copy(
                src_ref=chunk(src, b, p), dst_ref=chunk(dst, b, me),
                send_sem=src_sem.at[b], recv_sem=dst_sem.at[b],
                device_id=device, device_id_type=MESH,
            ).start()

        pltpu.make_async_copy(chunk(src, b, me), chunk(dst, b, me), dst_sem.at[b]).start()

    def arrived(dst, b, dst_sem):
        pltpu.make_async_copy(dst.at[b], dst.at[b], dst_sem.at[b]).wait()

    def departed(src, b, src_sem):
        part = src.at[b, pl.ds(0, (PEERS - 1) * CHUNK)]
        pltpu.make_async_copy(part, part, src_sem.at[b]).wait()

    channel = lax.broadcasted_iota(jnp.int32, (1, CHANNELS), 1)
    masks = [(channel // HEAD_DIM == h).astype(jnp.bfloat16) for h in range(HEADS)]
    key_head = lax.broadcasted_iota(jnp.int32, (512, CHANNELS), 0) // 16 % HEADS
    channel_head = lax.broadcasted_iota(jnp.int32, (512, CHANNELS), 1) // HEAD_DIM
    ones = (key_head == channel_head).astype(jnp.bfloat16)
    lane = lax.broadcasted_iota(jnp.int32, (64, 128), 1)

    def window_block(b, j):
        x = []
        for p in range(2):
            strips = [
                tokens[b * 8 + r, pl.ds(pl.multiple_of(32 * j + 16 * p, 16), 16), :].astype(jnp.float32)
                for r in range(8)
            ]
            x += [s[:8] for s in strips] + [s[8:] for s in strips]
        x = jnp.concatenate(x, axis=0)
        normed = layer_norm(x, gains[0:1])
        mixed = x + attention(normed, qkv_weight[0], out_weight[0], masks, ones, lane)
        mixed = mixed.astype(jnp.bfloat16).astype(jnp.float32)
        y = feed_forward(mixed, gains[1:2], up_weight[0], down_weight[0])
        for p in range(2):
            for r in range(8):
                lo, hi = 128 * p + 8 * r, 128 * p + 64 + 8 * r
                strip = jnp.concatenate([y[lo : lo + 8], y[hi : hi + 8]], axis=0)
                place = pl.ds(pl.multiple_of(128 * r + 32 * j + 16 * p, 16), 16)
                sent[b, place, :] = strip.astype(jnp.bfloat16)

    def grid_block(b, j):
        x = jnp.concatenate(
            [
                jnp.concatenate(
                    [regroup[h, pl.ds(4 * j + i, 64, stride=CHUNK), :] for h in range(2)], axis=1
                )
                for i in range(4)
            ],
            axis=0,
        )
        normed = layer_norm(x, gains[2:3])
        y = attention(normed, qkv_weight[1], out_weight[1], masks, ones, lane)
        for i in range(4):
            for h in range(2):
                ungroup[h, pl.ds(4 * j + i, 64, stride=CHUNK), :] = y[
                    64 * i : 64 * i + 64, 128 * h : 128 * h + 128
                ]

    def final_block(b, j):
        place = pl.ds(pl.multiple_of(BLOCK * j, BLOCK), BLOCK)
        mixed = sent[b, place, :].astype(jnp.float32) + back[b, place, :].astype(jnp.float32)
        mixed = mixed.astype(jnp.bfloat16).astype(jnp.float32)
        y = feed_forward(mixed, gains[3:4], up_weight[1], down_weight[1])
        out[pl.ds(b * 8 + 2 * j, 2), :, :] = y.astype(jnp.bfloat16).reshape(2, BREADTH, CHANNELS)

    blocks = BAND_TOKENS // BLOCK

    @pl.loop(0, BANDS + 4)
    def _(t):
        @pl.when(t < BANDS)
        def _():
            @pl.loop(0, blocks)
            def _(j):
                window_block(t, j)

            exchange(sent, recv, t, sent_sem, recv_sem)

        @pl.when((t >= 2) & (t < BANDS + 2))
        def _():
            b = t - 2
            arrived(recv, b, recv_sem)
            @pl.loop(0, blocks)
            def _(j):
                place = pl.ds(pl.multiple_of(BLOCK * j, BLOCK), BLOCK)
                for h in range(2):
                    regroup[h, place, :] = recv[b, place, 128 * h : 128 * h + 128].astype(jnp.float32)

            @pl.loop(0, blocks)
            def _(j):
                grid_block(b, j)

            @pl.loop(0, blocks)
            def _(j):
                place = pl.ds(pl.multiple_of(BLOCK * j, BLOCK), BLOCK)
                for h in range(2):
                    terms[b, place, 128 * h : 128 * h + 128] = ungroup[h, place, :].astype(jnp.bfloat16)

            exchange(terms, back, b, terms_sem, back_sem)

        @pl.when(t >= 4)
        def _():
            b = t - 4
            arrived(back, b, back_sem)
            @pl.loop(0, blocks)
            def _(j):
                final_block(b, j)

    @pl.loop(0, BANDS)
    def _(b):
        departed(sent, b, sent_sem)
        departed(terms, b, terms_sem)


def on_device(tokens, norm_gains, qkv_weight, out_weight, up_weight, down_weight):
    band = pltpu.VMEM((BANDS, BAND_TOKENS, CHANNELS), jnp.bfloat16)
    halves = pltpu.VMEM((2, BAND_TOKENS, 128), jnp.float32)
    return pl.pallas_call(
        kernel,
        out_shape=jax.ShapeDtypeStruct(tokens.shape, jnp.bfloat16),
        in_specs=[pl.BlockSpec(memory_space=pltpu.VMEM)] * 6,
        out_specs=pl.BlockSpec(memory_space=pltpu.VMEM),
        scratch_shapes=[band] * 4 + [halves] * 2 + [pltpu.SemaphoreType.DMA((BANDS,))] * 4,
        compiler_params=pltpu.CompilerParams(
            collective_id=0, has_side_effects=True, vmem_limit_bytes=56 * 2**20
        ),
    )(tokens, norm_gains, qkv_weight, out_weight, up_weight, down_weight)


def solution(mesh):
    return jax.shard_map(
        on_device,
        mesh=mesh,
        in_specs=(P("rows", "cols", None), P(), P(), P(), P(), P()),
        out_specs=P("rows", "cols", None),
        check_vma=False,
    )
```

profile of v0, /device:TPU:0, one launch (start us, length us, event | category | flops | bytes accessed | tf_op | source)
XLA Modules:
  0.0 144.6 jit_solution(4716958675617945489)
XLA Ops:
  0.0 141.5 %shard_map.64 = bf16[32,128,256]{2,1,0:T(8,128)(2,1)} custom-call(bf16[32,128,256]{2,1,0:T(8,128)(2,1)} %tokens.1, f32[4,256]{1,0:T(4,128)} %gains.1, bf16[2,256,768]{2,1,0:T(8,128)(2,1)} %qkv_weight.1, bf16[2,256,256]{2,1,0:T(8,128)(2,1)} %out_weight.1, bf16[2,256,1024]{2,1,0:T(8,128)(2,1)} %up_weight.1, bf16[2,1024,256]{2,1,0:T(8,128)(2,1)} %down_weight.1), custom_call_target="tpu_custom_call" | custom-call | tf_op jit(solution)/shard_map/pallas_call | solution.py:226
  141.5 3.1 %copy.8 = bf16[32,128,256]{2,1,0:T(8,128)(2,1)} copy(bf16[32,128,256]{2,1,0:T(8,128)(2,1)} %shard_map.64) | data formatting | bytes 4194304
where the time goes:
time: 145 us
  Pallas kernels  141 us (97%)
  local copies, waits for them, and re-layouts  3.13 us (2%)
    pallas_call x1, Pallas kernels, on_device(): pl.pallas_call(kernel, out_shape=jax.ShapeDtypeStruct(tokens.shape, jnp.b...  141 us
    unnamed x1, local copies, waits for them, and re-layouts  3.13 us

commit v1 on v0

--- a/solution.py
+++ b/solution.py
@@ -19,6 +19,9 @@
 PEERS = 64
 CHUNK = BAND_TOKENS // PEERS
 BLOCK = 256
+FINAL = 1024
+PAIRS = 8
+GROUPS = 16
 MESH = pl.DeviceIdType.MESH
 
 
@@ -52,13 +55,17 @@
     return x
 
 
-def attend(qkv, masks, ones, lane):
-    query = qkv[:, :CHANNELS]
-    keys = spread_heads(qkv[:, CHANNELS : 2 * CHANNELS], masks)
-    values = spread_heads(qkv[:, 2 * CHANNELS :], masks)
-    scores = lax.dot_general(
-        query, keys, (((1,), (1,)), ((), ())), preferred_element_type=jnp.float32
-    )
+def attention(normed, qkv_weight, out_weight, masks, ones, lane):
+    qkv = dot(normed, qkv_weight).astype(jnp.bfloat16)
+    groups = [slice(64 * w, 64 * w + 64) for w in range(normed.shape[0] // 64)]
+    keys = [spread_heads(qkv[g, CHANNELS : 2 * CHANNELS], masks) for g in groups]
+    scores = [
+        lax.dot_general(
+            qkv[g, :CHANNELS], k, (((1,), (1,)), ((), ())), preferred_element_type=jnp.float32
+        )
+        for g, k in zip(groups, keys)
+    ]
+    scores = jnp.concatenate(scores, axis=0)
     parts = [scores[:, 128 * t : 128 * t + 128] for t in range(4)]
     top = jnp.maximum(jnp.maximum(parts[0], parts[1]), jnp.maximum(parts[2], parts[3]))
     top = segment_max(top, lane)
@@ -66,15 +73,9 @@
         [jnp.exp2((p - top) * SCORE_SCALE).astype(jnp.bfloat16) for p in parts], axis=1
     )
     total = dot(weights, ones)
-    return (dot(weights, values) / total).astype(jnp.bfloat16)
-
-
-def attention(normed, qkv_weight, out_weight, masks, ones, lane):
-    qkv = dot(normed, qkv_weight).astype(jnp.bfloat16)
-    attended = [
-        attend(qkv[64 * w : 64 * w + 64], masks, ones, lane) for w in range(normed.shape[0] // 64)
-    ]
-    return dot(jnp.concatenate(attended, axis=0), out_weight)
+    values = [spread_heads(qkv[g, 2 * CHANNELS :], masks) for g in groups]
+    mixed = jnp.concatenate([dot(weights[g], v) for g, v in zip(groups, values)], axis=0)
+    return dot((mixed / total).astype(jnp.bfloat16), out_weight)
 
 
 def kernel(
@@ -125,13 +126,13 @@
     key_head = lax.broadcasted_iota(jnp.int32, (512, CHANNELS), 0) // 16 % HEADS
     channel_head = lax.broadcasted_iota(jnp.int32, (512, CHANNELS), 1) // HEAD_DIM
     ones = (key_head == channel_head).astype(jnp.bfloat16)
-    lane = lax.broadcasted_iota(jnp.int32, (64, 128), 1)
+    lane = lax.broadcasted_iota(jnp.int32, (1, 128), 1)
 
     def window_block(b, j):
         x = []
-        for p in range(2):
+        for p in range(PAIRS):
             strips = [
-                tokens[b * 8 + r, pl.ds(pl.multiple_of(32 * j + 16 * p, 16), 16), :].astype(jnp.float32)
+                tokens[b * 8 + r, pl.ds(pl.multiple_of(16 * (PAIRS * j + p), 16), 16), :].astype(jnp.float32)
                 for r in range(8)
             ]
             x += [s[:8] for s in strips] + [s[8:] for s in strips]
@@ -140,37 +141,37 @@
         mixed = x + attention(normed, qkv_weight[0], out_weight[0], masks, ones, lane)
         mixed = mixed.astype(jnp.bfloat16).astype(jnp.float32)
         y = feed_forward(mixed, gains[1:2], up_weight[0], down_weight[0])
-        for p in range(2):
+        for p in range(PAIRS):
             for r in range(8):
                 lo, hi = 128 * p + 8 * r, 128 * p + 64 + 8 * r
                 strip = jnp.concatenate([y[lo : lo + 8], y[hi : hi + 8]], axis=0)
-                place = pl.ds(pl.multiple_of(128 * r + 32 * j + 16 * p, 16), 16)
+                place = pl.ds(pl.multiple_of(128 * r + 16 * (PAIRS * j + p), 16), 16)
                 sent[b, place, :] = strip.astype(jnp.bfloat16)
 
     def grid_block(b, j):
         x = jnp.concatenate(
             [
                 jnp.concatenate(
-                    [regroup[h, pl.ds(4 * j + i, 64, stride=CHUNK), :] for h in range(2)], axis=1
+                    [regroup[h, pl.ds(GROUPS * j + i, 64, stride=CHUNK), :] for h in range(2)], axis=1
                 )
-                for i in range(4)
+                for i in range(GROUPS)
             ],
             axis=0,
         )
         normed = layer_norm(x, gains[2:3])
         y = attention(normed, qkv_weight[1], out_weight[1], masks, ones, lane)
-        for i in range(4):
+        for i in range(GROUPS):
             for h in range(2):
-                ungroup[h, pl.ds(4 * j + i, 64, stride=CHUNK), :] = y[
+                ungroup[h, pl.ds(GROUPS * j + i, 64, stride=CHUNK), :] = y[
                     64 * i : 64 * i + 64, 128 * h : 128 * h + 128
                 ]
 
     def final_block(b, j):
-        place = pl.ds(pl.multiple_of(BLOCK * j, BLOCK), BLOCK)
+        place = pl.ds(pl.multiple_of(FINAL * j, FINAL), FINAL)
         mixed = sent[b, place, :].astype(jnp.float32) + back[b, place, :].astype(jnp.float32)
         mixed = mixed.astype(jnp.bfloat16).astype(jnp.float32)
         y = feed_forward(mixed, gains[3:4], up_weight[1], down_weight[1])
-        out[pl.ds(b * 8 + 2 * j, 2), :, :] = y.astype(jnp.bfloat16).reshape(2, BREADTH, CHANNELS)
+        out[pl.ds(b * 8 + FINAL // BREADTH * j, FINAL // BREADTH), :, :] = y.astype(jnp.bfloat16).reshape(FINAL // BREADTH, BREADTH, CHANNELS)
 
     blocks = BAND_TOKENS // BLOCK
 
@@ -178,7 +179,7 @@
     def _(t):
         @pl.when(t < BANDS)
         def _():
-            @pl.loop(0, blocks)
+            @pl.loop(0, 8 // PAIRS)
             def _(j):
                 window_block(t, j)
 
@@ -194,7 +195,7 @@
                 for h in range(2):
                     regroup[h, place, :] = recv[b, place, 128 * h : 128 * h + 128].astype(jnp.float32)
 
-            @pl.loop(0, blocks)
+            @pl.loop(0, 16 // GROUPS)
             def _(j):
                 grid_block(b, j)
 
@@ -210,7 +211,7 @@
         def _():
             b = t - 4
             arrived(back, b, back_sem)
-            @pl.loop(0, blocks)
+            @pl.loop(0, BAND_TOKENS // FINAL)
             def _(j):
                 final_block(b, j)
 

time: 145 us -> 76.1 us (0.52)
  Pallas kernels: 141 us -> 72.8 us
    pallas_call x1, Pallas kernels: 141 us -> 72.8 us  [on_device(): pl.pallas_call(kernel, out_shape=jax.ShapeDtypeStruct(tokens.shape, jnp.b...]
where the time goes in v1:
time: 76.1 us; the launch traced here: 76 us
  Pallas kernels  72.8 us (96%)
  local copies, waits for them, and re-layouts  3.13 us (4%)
    pallas_call x1, Pallas kernels, on_device(): pl.pallas_call(kernel, out_shape=jax.ShapeDtypeStruct(tokens.shape, jnp.b...  72.8 us
    unnamed x1, local copies, waits for them, and re-layouts  3.13 us

profile of v1, /device:TPU:0, one launch (start us, length us, event | category | flops | bytes accessed | tf_op | source)
XLA Modules:
  0.0 76.0 jit_solution(9971972785690799238)
XLA Ops:
  0.0 72.8 %shard_map.64 = bf16[32,128,256]{2,1,0:T(8,128)(2,1)} custom-call(bf16[32,128,256]{2,1,0:T(8,128)(2,1)} %tokens.1, f32[4,256]{1,0:T(4,128)} %gains.1, bf16[2,256,768]{2,1,0:T(8,128)(2,1)} %qkv_weight.1, bf16[2,256,256]{2,1,0:T(8,128)(2,1)} %out_weight.1, bf16[2,256,1024]{2,1,0:T(8,128)(2,1)} %up_weight.1, bf16[2,1024,256]{2,1,0:T(8,128)(2,1)} %down_weight.1), custom_call_target="tpu_custom_call" | custom-call | tf_op jit(solution)/shard_map/pallas_call | solution.py:227
  72.8 3.1 %copy.8 = bf16[32,128,256]{2,1,0:T(8,128)(2,1)} copy(bf16[32,128,256]{2,1,0:T(8,128)(2,1)} %shard_map.64) | data formatting | bytes 4194304

commit v2 on v1

v2 whole, which is shorter than its diff:
```python
import math

import jax
import jax.numpy as jnp
from jax import lax
from jax.experimental import pallas as pl
from jax.experimental.pallas import tpu as pltpu
from jax.sharding import PartitionSpec as P

HEADS = 8
EPSILON = 1e-06
CHANNELS = 256
HEAD_DIM = CHANNELS // HEADS
SCORE_SCALE = math.log2(math.e) / math.sqrt(HEAD_DIM)
BANDS = 4
BAND_ROWS = 8
BREADTH = 128
BAND_TOKENS = BAND_ROWS * BREADTH
PEERS = 64
CHUNK = BAND_TOKENS // PEERS
WINDOW_STRAND = 512
GRID_STRAND = 512
FINAL_STRAND = 256
MESH = pl.DeviceIdType.MESH


def layer_norm(x, gain):
    centred = x - jnp.mean(x, axis=-1, keepdims=True)
    spread = jnp.mean(centred * centred, axis=-1, keepdims=True)
    return (centred * lax.rsqrt(spread + EPSILON) * gain).astype(jnp.bfloat16)


def dot(a, b):
    return jnp.dot(a, b, preferred_element_type=jnp.float32)


def interleave(strands):
    waiting, active = list(strands), []
    while waiting or active:
        if waiting:
            active.append(waiting.pop(0))
        for strand in list(active):
            if next(strand, strand) is strand:
                active.remove(strand)


def feed_forward(mix, gain, up, down):
    normed = layer_norm(mix, gain)
    yield
    twice = []
    for c in range(0, up.shape[1], 512):
        units = dot(normed, up[:, c : c + 512])
        twice.append((units + units * lax.erf(units * math.sqrt(0.5))).astype(jnp.bfloat16))
        yield
    return mix + 0.5 * dot(jnp.concatenate(twice, axis=1), down[...])


def spread_heads(x, masks):
    zero = jnp.zeros((16, 128), x.dtype)
    rows = []
    for t in range(4):
        low, high = x[16 * t : 16 * t + 16, :128], x[16 * t : 16 * t + 16, 128:]
        rows += [jnp.concatenate([low * m, zero], axis=1) for m in masks]
        rows += [jnp.concatenate([zero, high * m], axis=1) for m in masks]
    return jnp.concatenate(rows, axis=0)


def segment_max(x, lane, d=8):
    if d == 0:
        return x
    half = x.shape[0] // 2
    a, b = x[:half], x[half:]
    first = (lane & d) == 0
    both = jnp.where(
        first,
        jnp.maximum(a, pltpu.roll(a, 128 - d, 1)),
        jnp.maximum(b, pltpu.roll(b, d, 1)),
    )
    both = segment_max(both, lane, d // 2)
    return jnp.concatenate(
        [jnp.where(first, both, pltpu.roll(both, d, 1)), jnp.where(first, pltpu.roll(both, 128 - d, 1), both)],
        axis=0,
    )


def attention(normed, qkv_weight, out_weight, masks, ones, lane):
    qkv = dot(normed, qkv_weight[...]).astype(jnp.bfloat16)
    yield
    groups = [slice(64 * w, 64 * w + 64) for w in range(normed.shape[0] // 64)]
    scores = [
        lax.dot_general(
            qkv[g, :CHANNELS],
            spread_heads(qkv[g, CHANNELS : 2 * CHANNELS], masks),
            (((1,), (1,)), ((), ())),
            preferred_element_type=jnp.float32,
        )
        for g in groups
    ]
    scores = jnp.concatenate(scores, axis=0)
    parts = [scores[:, 128 * t : 128 * t + 128] for t in range(4)]
    top = jnp.maximum(jnp.maximum(parts[0], parts[1]), jnp.maximum(parts[2], parts[3]))
    yield
    top = segment_max(top, lane)
    yield
    weights = [jnp.exp2((p - top) * SCORE_SCALE) for p in parts]
    total = (weights[0] + weights[1]) + (weights[2] + weights[3])
    coarse = total.astype(jnp.bfloat16)
    fine = (total - coarse.astype(jnp.float32)).astype(jnp.bfloat16)
    total = dot(jnp.concatenate([coarse, fine], axis=1), ones)
    weights = jnp.concatenate([w.astype(jnp.bfloat16) for w in weights], axis=1)
    yield
    mixed = [
        dot(weights[g], spread_heads(qkv[g, 2 * CHANNELS :], masks)) for g in groups
    ]
    mixed = (jnp.concatenate(mixed, axis=0) / total).astype(jnp.bfloat16)
    yield
    return dot(mixed, out_weight[...])


def kernel(
    tokens_hbm, gains_hbm, qkv_hbm, out_hbm, up_hbm, down_hbm, result_hbm,
    tokens, gains, qkv_weight, out_weight, up_weight, down_weight, result,
    sent, recv, terms, back, regroup, ungroup,
    token_sem, gain_sem, weight_sem, result_sem, sent_sem, recv_sem, terms_sem, back_sem,
):
    row, col = lax.axis_index("rows"), lax.axis_index("cols")
    core, place_row = lax.rem(row, 2), lax.div(row, 2)
    me = place_row * 8 + col

    def load_tokens(b):
        rows = pl.ds(b * BAND_ROWS, BAND_ROWS)
        return pltpu.make_async_copy(tokens_hbm.at[rows], tokens.at[rows], token_sem.at[b])

    def load_weights(i):
        pairs = ((qkv_hbm, qkv_weight), (out_hbm, out_weight), (up_hbm, up_weight), (down_hbm, down_weight))
        return [
            pltpu.make_async_copy(src.at[i], dst.at[i], weight_sem.at[i, n])
            for n, (src, dst) in enumerate(pairs)
        ]

    def store_result(b):
        rows = pl.ds(b * BAND_ROWS, BAND_ROWS)
        return pltpu.make_async_copy(result.at[rows], result_hbm.at[rows], result_sem.at[b])

    load_gains = pltpu.make_async_copy(gains_hbm, gains, gain_sem)
    load_gains.start()
    load_tokens(0).start()
    for copy in load_weights(0):
        copy.start()
    for b in range(1, BANDS):
        load_tokens(b).start()
    for copy in load_weights(1):
        copy.start()

    peer_cols = [lax.rem(col + c, 8) for c in range(8)]

    def each_peer(act):
        @pl.loop(0, 8)
        def _(a):
            r = lax.rem(place_row + a, 8)
            for c in range(1, 8):
                act(r * 8 + peer_cols[c], (2 * r + core, peer_cols[c]))

        @pl.loop(1, 8)
        def _(a):
            r = lax.rem(place_row + a, 8)
            act(r * 8 + col, (2 * r + core, col))

    barrier = pltpu.get_barrier_semaphore()
    each_peer(
        lambda p, device: pl.semaphore_signal(barrier, inc=1, device_id=device, device_id_type=MESH)
    )

    def chunk(ref, b, p):
        return ref.at[b, pl.ds(pl.multiple_of(p * CHUNK, CHUNK), CHUNK)]

    def exchange(src, dst, b, src_sem, dst_sem):
        each_peer(
            lambda p, device: pltpu.make_async_remote_copy(
                src_ref=chunk(src, b, p), dst_ref=chunk(dst, b, me),
                send_sem=src_sem.at[b], recv_sem=dst_sem.at[b],
                device_id=device, device_id_type=MESH,
            ).start()
        )
        pltpu.make_async_copy(chunk(src, b, me), chunk(dst, b, me), dst_sem.at[b]).start()

    def arrived(dst, b, dst_sem):
        pltpu.make_async_copy(dst.at[b], dst.at[b], dst_sem.at[b]).wait()

    def departed(src, b, src_sem):
        part = src.at[b, pl.ds(0, (PEERS - 1) * CHUNK)]
        pltpu.make_async_copy(part, part, src_sem.at[b]).wait()

    channel = lax.broadcasted_iota(jnp.int32, (1, 128), 1)
    masks = [(channel // HEAD_DIM == j).astype(jnp.bfloat16) for j in range(4)]
    key_head = lax.broadcasted_iota(jnp.int32, (CHANNELS, CHANNELS), 0) // 16 % HEADS
    channel_head = lax.broadcasted_iota(jnp.int32, (CHANNELS, CHANNELS), 1) // HEAD_DIM
    ones = (key_head == channel_head).astype(jnp.bfloat16)
    lane = lax.broadcasted_iota(jnp.int32, (1, 128), 1)

    def window_strand(b, first):
        pairs = range(first // 128, (first + WINDOW_STRAND) // 128)
        x = []
        for p in pairs:
            strips = [
                tokens[b * BAND_ROWS + r, 16 * p : 16 * p + 16, :].astype(jnp.float32) for r in range(8)
            ]
            x += [s[:8] for s in strips] + [s[8:] for s in strips]
        x = jnp.concatenate(x, axis=0)
        normed = layer_norm(x, gains[0:1])
        yield
        terms_a = yield from attention(normed, qkv_weight.at[0], out_weight.at[0], masks, ones, lane)
        mixed = (x + terms_a).astype(jnp.bfloat16).astype(jnp.float32)
        yield
        y = yield from feed_forward(mixed, gains[1:2], up_weight.at[0], down_weight.at[0])
        for n, p in enumerate(pairs):
            for r in range(8):
                lo, hi = 128 * n + 8 * r, 128 * n + 64 + 8 * r
                strip = jnp.concatenate([y[lo : lo + 8], y[hi : hi + 8]], axis=0)
                sent[b, 128 * r + 16 * p : 128 * r + 16 * p + 16, :] = strip.astype(jnp.bfloat16)

    def grid_strand(first):
        members = range(first // 64, (first + GRID_STRAND) // 64)
        x = jnp.concatenate(
            [
                jnp.concatenate([regroup[h, pl.ds(g, 64, stride=CHUNK), :] for h in range(2)], axis=1)
                for g in members
            ],
            axis=0,
        )
        normed = layer_norm(x, gains[2:3])
        yield
        y = yield from attention(normed, qkv_weight.at[1], out_weight.at[1], masks, ones, lane)
        for n, g in enumerate(members):
            for h in range(2):
                ungroup[h, pl.ds(g, 64, stride=CHUNK), :] = y[
                    64 * n : 64 * n + 64, 128 * h : 128 * h + 128
                ]

    def final_strand(b, first):
        span = pl.ds(first, FINAL_STRAND)
        mixed = sent[b, span, :].astype(jnp.float32) + back[b, span, :].astype(jnp.float32)
        mixed = mixed.astype(jnp.bfloat16).astype(jnp.float32)
        yield
        y = yield from feed_forward(mixed, gains[3:4], up_weight.at[1], down_weight.at[1])
        rows = FINAL_STRAND // BREADTH
        result[pl.ds(b * BAND_ROWS + first // BREADTH, rows), :, :] = y.astype(jnp.bfloat16).reshape(
            rows, BREADTH, CHANNELS
        )

    @pl.loop(0, BANDS + 4)
    def _(t):
        @pl.when(t == 0)
        def _():
            load_gains.wait()
            for copy in load_weights(0):
                copy.wait()

        @pl.when(t < BANDS)
        def _():
            load_tokens(t).wait()
            interleave(window_strand(t, f) for f in range(0, BAND_TOKENS, WINDOW_STRAND))

        @pl.when(t == 0)
        def _():
            pl.semaphore_wait(barrier, PEERS - 1)
            for copy in load_weights(1):
                copy.wait()

        @pl.when(t < BANDS)
        def _():
            exchange(sent, recv, t, sent_sem, recv_sem)

        @pl.when((t >= 2) & (t < BANDS + 2))
        def _():
            b = t - 2
            arrived(recv, b, recv_sem)
            for h in range(2):
                regroup[h] = recv[b, :, 128 * h : 128 * h + 128].astype(jnp.float32)
            interleave(grid_strand(f) for f in range(0, BAND_TOKENS, GRID_STRAND))
            for h in range(2):
                terms[b, :, 128 * h : 128 * h + 128] = ungroup[h].astype(jnp.bfloat16)
            exchange(terms, back, b, terms_sem, back_sem)

        @pl.when(t >= 4)
        def _():
            b = t - 4
            arrived(back, b, back_sem)
            interleave(final_strand(b, f) for f in range(0, BAND_TOKENS, FINAL_STRAND))
            store_result(b).start()

    @pl.loop(0, BANDS)
    def _(b):
        departed(sent, b, sent_sem)
        departed(terms, b, terms_sem)
        store_result(b).wait()


def on_device(tokens, norm_gains, qkv_weight, out_weight, up_weight, down_weight):
    arrays = (tokens, norm_gains, qkv_weight, out_weight, up_weight, down_weight)
    band = pltpu.VMEM((BANDS, BAND_TOKENS, CHANNELS), jnp.bfloat16)
    halves = pltpu.VMEM((2, BAND_TOKENS, 128), jnp.float32)
    return pl.pallas_call(
        kernel,
        out_shape=jax.ShapeDtypeStruct(tokens.shape, jnp.bfloat16),
        in_specs=[pl.BlockSpec(memory_space=pl.ANY)] * 6,
        out_specs=pl.BlockSpec(memory_space=pl.ANY),
        scratch_shapes=[pltpu.VMEM(a.shape, a.dtype) for a in arrays]
        + [pltpu.VMEM(tokens.shape, jnp.bfloat16)]
        + [band] * 4
        + [halves] * 2
        + [
            pltpu.SemaphoreType.DMA((BANDS,)),
            pltpu.SemaphoreType.DMA,
            pltpu.SemaphoreType.DMA((2, 4)),
        ]
        + [pltpu.SemaphoreType.DMA((BANDS,))] * 5,
        compiler_params=pltpu.CompilerParams(
            collective_id=0, has_side_effects=True, vmem_limit_bytes=56 * 2**20
        ),
    )(*arrays)


def solution(mesh):
    return jax.shard_map(
        on_device,
        mesh=mesh,
        in_specs=(P("rows", "cols", None), P(), P(), P(), P(), P()),
        out_specs=P("rows", "cols", None),
        check_vma=False,
    )
```

time: 76.1 us -> 75.5 us (level)
  the two profiles are of different devices: /device:TPU:0 before, /device:TPU:24 now
where the time goes in v2:
time: 75.5 us; the launch traced here: 75.4 us
  Pallas kernels  72.2 us (96%)
  local copies, waits for them, and re-layouts  3.13 us (4%)
    pallas_call x1, Pallas kernels, on_device(): pl.pallas_call(kernel, out_shape=jax.ShapeDtypeStruct(tokens.shape, jnp.b...  72.2 us
    unnamed x1, local copies, waits for them, and re-layouts  3.13 us

profile of v2, /device:TPU:24, one launch (start us, length us, event | category | flops | bytes accessed | tf_op | source)
XLA Modules:
  0.0 75.4 jit_solution(1346755363835447700)
XLA Ops:
  0.0 72.2 %shard_map.64 = bf16[32,128,256]{2,1,0:T(8,128)(2,1)} custom-call(bf16[32,128,256]{2,1,0:T(8,128)(2,1)} %tokens_hbm.1, f32[4,256]{1,0:T(4,128)} %gains_hbm.1, bf16[2,256,768]{2,1,0:T(8,128)(2,1)} %qkv_hbm.1, bf16[2,256,256]{2,1,0:T(8,128)(2,1)} %out_hbm.1, bf16[2,256,1024]{2,1,0:T(8,128)(2,1)} %up_hbm.1, bf16[2,1024,256]{2,1,0:T(8,128)(2,1)} %down_hbm.1), custom_call_target="tpu_custom_call" | custom-call | tf_op jit(solution)/shard_map/pallas_call | solution.py:303
  72.2 3.1 %copy.8 = bf16[32,128,256]{2,1,0:T(8,128)(2,1)} copy(bf16[32,128,256]{2,1,0:T(8,128)(2,1)} %shard_map.64) | data formatting | bytes 4194304

commit v3 on v2

--- a/solution.py
+++ b/solution.py
@@ -52,7 +52,7 @@
         units = dot(normed, up[:, c : c + 512])
         twice.append((units + units * lax.erf(units * math.sqrt(0.5))).astype(jnp.bfloat16))
         yield
-    return mix + 0.5 * dot(jnp.concatenate(twice, axis=1), down[...])
+    return (mix + mix) + dot(jnp.concatenate(twice, axis=1), down[...])
 
 
 def spread_heads(x, masks):
@@ -118,10 +118,10 @@
 
 
 def kernel(
-    tokens_hbm, gains_hbm, qkv_hbm, out_hbm, up_hbm, down_hbm, result_hbm,
-    tokens, gains, qkv_weight, out_weight, up_weight, down_weight, result,
+    tokens_hbm, gains_hbm, qkv_hbm, out_hbm, up_hbm, down_hbm, result,
+    tokens, gains, qkv_weight, out_weight, up_weight, down_weight,
     sent, recv, terms, back, regroup, ungroup,
-    token_sem, gain_sem, weight_sem, result_sem, sent_sem, recv_sem, terms_sem, back_sem,
+    token_sem, gain_sem, weight_sem, sent_sem, recv_sem, terms_sem, back_sem,
 ):
     row, col = lax.axis_index("rows"), lax.axis_index("cols")
     core, place_row = lax.rem(row, 2), lax.div(row, 2)
@@ -137,10 +137,6 @@
             pltpu.make_async_copy(src.at[i], dst.at[i], weight_sem.at[i, n])
             for n, (src, dst) in enumerate(pairs)
         ]
-
-    def store_result(b):
-        rows = pl.ds(b * BAND_ROWS, BAND_ROWS)
-        return pltpu.make_async_copy(result.at[rows], result_hbm.at[rows], result_sem.at[b])
 
     load_gains = pltpu.make_async_copy(gains_hbm, gains, gain_sem)
     load_gains.start()
@@ -182,10 +178,12 @@
                 device_id=device, device_id_type=MESH,
             ).start()
         )
-        pltpu.make_async_copy(chunk(src, b, me), chunk(dst, b, me), dst_sem.at[b]).start()
+        own = pl.ds(pl.multiple_of(me * CHUNK, CHUNK), CHUNK)
+        dst[b, own, :] = src[b, own, :]
 
     def arrived(dst, b, dst_sem):
-        pltpu.make_async_copy(dst.at[b], dst.at[b], dst_sem.at[b]).wait()
+        part = dst.at[b, pl.ds(0, (PEERS - 1) * CHUNK)]
+        pltpu.make_async_copy(part, part, dst_sem.at[b]).wait()
 
     def departed(src, b, src_sem):
         part = src.at[b, pl.ds(0, (PEERS - 1) * CHUNK)]
@@ -216,7 +214,7 @@
         for n, p in enumerate(pairs):
             for r in range(8):
                 lo, hi = 128 * n + 8 * r, 128 * n + 64 + 8 * r
-                strip = jnp.concatenate([y[lo : lo + 8], y[hi : hi + 8]], axis=0)
+                strip = 0.5 * jnp.concatenate([y[lo : lo + 8], y[hi : hi + 8]], axis=0)
                 sent[b, 128 * r + 16 * p : 128 * r + 16 * p + 16, :] = strip.astype(jnp.bfloat16)
 
     def grid_strand(first):
@@ -271,9 +269,9 @@
         def _():
             exchange(sent, recv, t, sent_sem, recv_sem)
 
-        @pl.when((t >= 2) & (t < BANDS + 2))
-        def _():
-            b = t - 2
+        @pl.when((t == 1) | ((t >= 3) & (t < BANDS + 2)))
+        def _():
+            b = jnp.where(t < 2, 0, t - 2)
             arrived(recv, b, recv_sem)
             for h in range(2):
                 regroup[h] = recv[b, :, 128 * h : 128 * h + 128].astype(jnp.float32)
@@ -287,26 +285,23 @@
             b = t - 4
             arrived(back, b, back_sem)
             interleave(final_strand(b, f) for f in range(0, BAND_TOKENS, FINAL_STRAND))
-            store_result(b).start()
 
     @pl.loop(0, BANDS)
     def _(b):
         departed(sent, b, sent_sem)
         departed(terms, b, terms_sem)
-        store_result(b).wait()
 
 
 def on_device(tokens, norm_gains, qkv_weight, out_weight, up_weight, down_weight):
     arrays = (tokens, norm_gains, qkv_weight, out_weight, up_weight, down_weight)
     band = pltpu.VMEM((BANDS, BAND_TOKENS, CHANNELS), jnp.bfloat16)
     halves = pltpu.VMEM((2, BAND_TOKENS, 128), jnp.float32)
-    return pl.pallas_call(
+    twice = pl.pallas_call(
         kernel,
-        out_shape=jax.ShapeDtypeStruct(tokens.shape, jnp.bfloat16),
+        out_shape=pltpu.VMEM(tokens.shape, jnp.bfloat16),
         in_specs=[pl.BlockSpec(memory_space=pl.ANY)] * 6,
-        out_specs=pl.BlockSpec(memory_space=pl.ANY),
+        out_specs=pl.BlockSpec(memory_space=pltpu.VMEM),
         scratch_shapes=[pltpu.VMEM(a.shape, a.dtype) for a in arrays]
-        + [pltpu.VMEM(tokens.shape, jnp.bfloat16)]
         + [band] * 4
         + [halves] * 2
         + [
@@ -314,11 +309,12 @@
             pltpu.SemaphoreType.DMA,
             pltpu.SemaphoreType.DMA((2, 4)),
         ]
-        + [pltpu.SemaphoreType.DMA((BANDS,))] * 5,
+        + [pltpu.SemaphoreType.DMA((BANDS,))] * 4,
         compiler_params=pltpu.CompilerParams(
-            collective_id=0, has_side_effects=True, vmem_limit_bytes=56 * 2**20
+            collective_id=0, has_side_effects=True, vmem_limit_bytes=60 * 2**20
         ),
     )(*arrays)
+    return twice * 0.5
 
 
 def solution(mesh):

time: 75.5 us -> 69 us (0.914)
  the two profiles are of different devices: /device:TPU:24 before, /device:TPU:0 now
where the time goes in v3:
time: 69 us; the launch traced here: 68.9 us
  Pallas kernels  67.4 us (98%)
  other arithmetic  1.5 us (2%)
    pallas_call x1, Pallas kernels, on_device(): pl.pallas_call(kernel, out_shape=pltpu.VMEM(tokens.shape, jnp.bfloat16),...  67.4 us
    mul x1, other arithmetic, on_device(): return twice * 0.5  1.5 us

profile of v3, /device:TPU:0, one launch (start us, length us, event | category | flops | bytes accessed | tf_op | source)
XLA Modules:
  0.0 68.9 jit_solution(15452456329226703046)
XLA Ops:
  0.0 67.4 %shard_map.64 = bf16[32,128,256]{2,1,0:T(8,128)(2,1)S(1)} custom-call(bf16[32,128,256]{2,1,0:T(8,128)(2,1)} %tokens_hbm.1, f32[4,256]{1,0:T(4,128)} %gains_hbm.1, bf16[2,256,768]{2,1,0:T(8,128)(2,1)} %qkv_hbm.1, bf16[2,256,256]{2,1,0:T(8,128)(2,1)} %out_hbm.1, bf16[2,256,1024]{2,1,0:T(8,128)(2,1)} %up_hbm.1, bf16[2,1024,256]{2,1,0:T(8,128)(2,1)} %down_hbm.1), custom_call_target="tpu_custom_call" | custom-call | tf_op jit(solution)/shard_map/pallas_call | solution.py:299
  67.4 1.5 %broadcast_multiply_fusion = bf16[32,128,256]{2,1,0:T(8,128)(2,1)} fusion(bf16[32,128,256]{2,1,0:T(8,128)(2,1)S(1)} %shard_map.64), kind=kLoop, calls=%fused_computation | loop fusion | flops 1048576 | bytes 4194304 | tf_op jit(solution)/shard_map/mul | solution.py:317

commit v4 on v3

--- a/solution.py
+++ b/solution.py
@@ -106,9 +106,9 @@
     total = (weights[0] + weights[1]) + (weights[2] + weights[3])
     coarse = total.astype(jnp.bfloat16)
     fine = (total - coarse.astype(jnp.float32)).astype(jnp.bfloat16)
+    weights = jnp.concatenate([w.astype(jnp.bfloat16) for w in weights], axis=1)
+    yield
     total = dot(jnp.concatenate([coarse, fine], axis=1), ones)
-    weights = jnp.concatenate([w.astype(jnp.bfloat16) for w in weights], axis=1)
-    yield
     mixed = [
         dot(weights[g], spread_heads(qkv[g, 2 * CHANNELS :], masks)) for g in groups
     ]
@@ -143,24 +143,14 @@
     load_tokens(0).start()
     for copy in load_weights(0):
         copy.start()
-    for b in range(1, BANDS):
-        load_tokens(b).start()
-    for copy in load_weights(1):
-        copy.start()
-
     peer_cols = [lax.rem(col + c, 8) for c in range(8)]
 
     def each_peer(act):
-        @pl.loop(0, 8)
-        def _(a):
+        for a in range(8):
             r = lax.rem(place_row + a, 8)
-            for c in range(1, 8):
-                act(r * 8 + peer_cols[c], (2 * r + core, peer_cols[c]))
-
-        @pl.loop(1, 8)
-        def _(a):
-            r = lax.rem(place_row + a, 8)
-            act(r * 8 + col, (2 * r + core, col))
+            for c in range(8):
+                if a + c > 0:
+                    act(r * 8 + peer_cols[c], (2 * r + core, peer_cols[c]))
 
     barrier = pltpu.get_barrier_semaphore()
     each_peer(
@@ -253,6 +243,10 @@
             load_gains.wait()
             for copy in load_weights(0):
                 copy.wait()
+            for b in range(1, BANDS):
+                load_tokens(b).start()
+            for copy in load_weights(1):
+                copy.start()
 
         @pl.when(t < BANDS)
         def _():

time: 69 us -> 65.7 us (0.952)
  Pallas kernels: 67.4 us -> 63.9 us
    pallas_call x1, Pallas kernels: 67.4 us -> 63.9 us  [on_device(): pl.pallas_call(kernel, out_shape=pltpu.VMEM(tokens.shape, jnp.bfloat16),...]
where the time goes in v4:
time: 65.7 us; the launch traced here: 65.5 us
  Pallas kernels  63.9 us (97%)
  other arithmetic  1.5 us (2%)
    pallas_call x1, Pallas kernels, on_device(): pl.pallas_call(kernel, out_shape=pltpu.VMEM(tokens.shape, jnp.bfloat16),...  63.9 us
    mul x1, other arithmetic, on_device(): return twice * 0.5  1.5 us

profile of v4, /device:TPU:0, one launch (start us, length us, event | category | flops | bytes accessed | tf_op | source)
XLA Modules:
  0.0 65.5 jit_solution(4285055479810605933)
XLA Ops:
  0.0 63.9 %shard_map.64 = bf16[32,128,256]{2,1,0:T(8,128)(2,1)S(1)} custom-call(bf16[32,128,256]{2,1,0:T(8,128)(2,1)} %tokens_hbm.1, f32[4,256]{1,0:T(4,128)} %gains_hbm.1, bf16[2,256,768]{2,1,0:T(8,128)(2,1)} %qkv_hbm.1, bf16[2,256,256]{2,1,0:T(8,128)(2,1)} %out_hbm.1, bf16[2,256,1024]{2,1,0:T(8,128)(2,1)} %up_hbm.1, bf16[2,1024,256]{2,1,0:T(8,128)(2,1)} %down_hbm.1), custom_call_target="tpu_custom_call" | custom-call | tf_op jit(solution)/shard_map/pallas_call | solution.py:293
  64.0 1.5 %broadcast_multiply_fusion = bf16[32,128,256]{2,1,0:T(8,128)(2,1)} fusion(bf16[32,128,256]{2,1,0:T(8,128)(2,1)S(1)} %shard_map.64), kind=kLoop, calls=%fused_computation | loop fusion | flops 1048576 | bytes 4194304 | tf_op jit(solution)/shard_map/mul | solution.py:311

commit v5 on v4

--- a/solution.py
+++ b/solution.py
@@ -236,7 +236,7 @@
             rows, BREADTH, CHANNELS
         )
 
-    @pl.loop(0, BANDS + 4)
+    @pl.loop(0, BANDS + 5)
     def _(t):
         @pl.when(t == 0)
         def _():
@@ -274,9 +274,9 @@
                 terms[b, :, 128 * h : 128 * h + 128] = ungroup[h].astype(jnp.bfloat16)
             exchange(terms, back, b, terms_sem, back_sem)
 
-        @pl.when(t >= 4)
-        def _():
-            b = t - 4
+        @pl.when(t >= 5)
+        def _():
+            b = t - 5
             arrived(back, b, back_sem)
             interleave(final_strand(b, f) for f in range(0, BAND_TOKENS, FINAL_STRAND))
 

time: 65.7 us -> 65.7 us (level)
  no operation moved by 1% of the time
where the time goes in v5:
time: 65.7 us; the launch traced here: 65.5 us
  Pallas kernels  63.9 us (97%)
  other arithmetic  1.5 us (2%)
    pallas_call x1, Pallas kernels, on_device(): pl.pallas_call(kernel, out_shape=pltpu.VMEM(tokens.shape, jnp.bfloat16),...  63.9 us
    mul x1, other arithmetic, on_device(): return twice * 0.5  1.5 us

profile of v5, /device:TPU:0, one launch (start us, length us, event | category | flops | bytes accessed | tf_op | source)
XLA Modules:
  0.0 65.5 jit_solution(18163859746957769392)
XLA Ops:
  0.0 63.9 %shard_map.64 = bf16[32,128,256]{2,1,0:T(8,128)(2,1)S(1)} custom-call(bf16[32,128,256]{2,1,0:T(8,128)(2,1)} %tokens_hbm.1, f32[4,256]{1,0:T(4,128)} %gains_hbm.1, bf16[2,256,768]{2,1,0:T(8,128)(2,1)} %qkv_hbm.1, bf16[2,256,256]{2,1,0:T(8,128)(2,1)} %out_hbm.1, bf16[2,256,1024]{2,1,0:T(8,128)(2,1)} %up_hbm.1, bf16[2,1024,256]{2,1,0:T(8,128)(2,1)} %down_hbm.1), custom_call_target="tpu_custom_call" | custom-call | tf_op jit(solution)/shard_map/pallas_call | solution.py:293
  64.0 1.5 %broadcast_multiply_fusion = bf16[32,128,256]{2,1,0:T(8,128)(2,1)} fusion(bf16[32,128,256]{2,1,0:T(8,128)(2,1)S(1)} %shard_map.64), kind=kLoop, calls=%fused_computation | loop fusion | flops 1048576 | bytes 4194304 | tf_op jit(solution)/shard_map/mul | solution.py:311
